TPU v7x, 32 devices: a whole 2x2x4 slice. The times are simulated.
32 devices in a mesh: grp: 2 (over y), ep: 8 (over z, core), tp: 2 (over x).
Axes of the slice: x: 2, y: 2, z: 4, core: 2. Of those that a mesh axis runs over, the one named last changes fastest.
Arguments:
- queries: bfloat16 [1024, 8192], P(('grp', 'ep'), 'tp'), parts along dimension 0, may hold values from -6 to 6
- draft_kv: bfloat16 [1024, 512], P(('grp', 'ep')), parts along dimension 0, may hold values from -6 to 6
- kv_cache: bfloat16 [256, 256, 512], P(('grp', 'ep', 'tp')), parts along dimension 0, may hold values from -6 to 6
- lengths: int32 [256], P(('grp', 'ep')), parts along dimension 0, may hold values from 1 to 256, as said below
- residual: bfloat16 [1024, 3584], P(('grp', 'ep', 'tp')), parts along dimension 0, may hold values from -6 to 6
- out_proj: bfloat16 [8192, 3584], P('tp'), may hold values from -0.5 to 0.5
- norm_gain: float32 [3584], replicated, may hold values from 0.1 to 1.9
- up_proj: bfloat16 [8, 3584, 2560], P('ep', None, 'tp'), may hold values from -0.09375 to 0.09375
- down_proj: bfloat16 [8, 2560, 3584], P('ep', 'tp'), may hold values from -0.125 to 0.125
- routes: int32 [1024, 3], P(('grp', 'ep', 'tp')), parts along dimension 0, may hold values from 0 to 7, all different within a row; in each aligned block of 32 rows (0 to 31, 32 to 63, ...) at most 12 rows name the same one
- route_gates: float32 [1024, 3], P(('grp', 'ep', 'tp')), parts along dimension 0, may hold values from 0.2 to 1
- lost_device: int32 [2], P('grp'), parts along dimension 0, may hold values from 0 to 7
- spare_table: int32 [16], P('grp'), parts along dimension 0, may hold values from 0 to 7, as said below
Outputs:
- layer_out: bfloat16 [1024, 3584], P(('grp', 'ep', 'tp')), parts along dimension 0
There are 2 independent parts, one for each index of `grp`. A program takes and returns all parts, laid end to end along the dimension named above; an argument that names none is the same for every part. Nothing has to cross between parts.
Inputs may be any that keep to these rules, and one draw needn't show every extreme that they name: lengths reach 256 in every draw. `routes`: each row names 3 different experts; in the rows of one device (aligned blocks of 32 rows) no expert is named by more than 12 rows. `spare_table`: no entry equals its own index.
All inputs are finite; a program needn't handle non-finite values.
Results may differ from a plain program's by a relative error of at most 0.013.
Values may be sent and summed in bfloat16 or wider, within the bound.
A program may use at most 192 MiB of HBM per device.

v0:
```python
import math

import jax
import jax.numpy as jnp
from jax import lax
from jax.sharding import PartitionSpec as P

EPSILON = 1e-06


def shards(
    queries,
    draft_kv,
    kv_cache,
    lengths,
    residual,
    out_proj,
    norm_gain,
    up_proj,
    down_proj,
    routes,
    route_gates,
    lost_device,
    spare_table,
):
    requests = lengths.shape[0]
    drafts = draft_kv.shape[0] // requests
    head_dim = draft_kv.shape[1] // 2
    head_count = queries.shape[1] // head_dim
    factor = 1.0 / math.sqrt(head_dim)
    query_heads = queries.reshape(requests, drafts, head_count, head_dim)
    draft_rows = draft_kv.reshape(requests, drafts, 2 * head_dim)
    draft_order = jnp.arange(drafts)
    block_rows = lax.all_gather(kv_cache, "tp", axis=0, tiled=True)
    amount = block_rows.shape[0]
    cached = block_rows.shape[1]
    key_rows = jnp.concatenate([block_rows[:, :, :head_dim], draft_rows[:, :, :head_dim]], 1)
    value_rows = jnp.concatenate([block_rows[:, :, head_dim:], draft_rows[:, :, head_dim:]], 1)
    scores = (
        jnp.einsum("rthd,rkd->rthk", query_heads, key_rows, preferred_element_type=jnp.float32)
        * factor
    )
    position = jnp.arange(cached + drafts)
    visible = jnp.where(
        position[None, None, :] < cached,
        position[None, None, :] < lengths[:, None, None],
        position[None, None, :] - cached <= draft_order[None, :, None],
    )
    visible = visible[:, :, None, :]
    peak = jnp.max(jnp.where(visible, scores, -jnp.inf), axis=-1, keepdims=True)
    weights = jnp.where(visible, jnp.exp(scores - peak), 0.0)
    totals = jnp.sum(weights, axis=-1, keepdims=True)
    mixture = (
        jnp.einsum(
            "rthk,rkd->rthd",
            weights.astype(jnp.bfloat16),
            value_rows,
            preferred_element_type=jnp.float32,
        )
        / totals
    )
    attended = mixture.astype(jnp.bfloat16).reshape(amount * drafts, head_count * head_dim)
    kept_rows = residual.shape[0]
    features = residual.shape[1]
    summed = lax.psum_scatter(
        jnp.dot(attended, out_proj, preferred_element_type=jnp.float32).astype(jnp.bfloat16),
        "tp",
        scatter_dimension=0,
        tiled=True,
    ).astype(jnp.float32)
    hidden = (residual.astype(jnp.float32) + summed).astype(jnp.bfloat16)
    widened = hidden.astype(jnp.float32)
    normed = (
        widened
        * lax.rsqrt(jnp.mean(widened * widened, axis=-1, keepdims=True) + EPSILON)
        * norm_gain
    ).astype(jnp.bfloat16)
    experts = lax.axis_size("ep")
    tp_lanes = lax.axis_size("tp")
    per_row = routes.shape[1]
    capacity = min(kept_rows, (kept_rows * per_row + experts - 1) // experts)
    lost_id = lost_device[0]
    spare_id = jnp.sum(jnp.where(jnp.arange(experts) == lost_id, spare_table, 0))
    flat_routes = routes.reshape(-1)
    is_lost = flat_routes == lost_id
    lost_count = is_lost.astype(jnp.int32)
    earlier_lost = jnp.cumsum(lost_count) - lost_count
    one_hot = (flat_routes[:, None] == jnp.arange(experts)[None, :]).astype(jnp.int32)
    earlier_same = jnp.sum((jnp.cumsum(one_hot, axis=0) - one_hot) * one_hot, axis=1)
    slot_count = 2 * capacity
    target = jnp.where(is_lost, spare_id, flat_routes)
    slot_place = jnp.where(is_lost, capacity + earlier_lost, earlier_same)
    spare_up, spare_down = (up_proj, down_proj)
    slot_index = target * slot_count + slot_place
    selector = (slot_index[None, :] == jnp.arange(experts * slot_count)[:, None]).astype(
        jnp.bfloat16
    )
    repeated = jnp.repeat(normed, per_row, axis=0)
    outgoing = jnp.dot(selector, repeated, preferred_element_type=jnp.float32).astype(jnp.bfloat16)
    outgoing = outgoing.reshape(experts, slot_count, features)
    copies = jnp.broadcast_to(outgoing[:, None], (experts, tp_lanes, slot_count, features))
    copies = copies.reshape(experts * tp_lanes, slot_count, features)
    arrived = lax.all_to_all(copies, ("ep", "tp"), split_axis=0, concat_axis=0, tiled=True)
    main_part = jnp.einsum(
        "nsd,df->nsf", arrived[:, :capacity], up_proj[0], preferred_element_type=jnp.float32
    )
    spare_part = jnp.einsum(
        "nsd,df->nsf", arrived[:, capacity:], spare_up[0], preferred_element_type=jnp.float32
    )
    main_out = jnp.einsum(
        "nsf,fd->nsd",
        jax.nn.silu(main_part).astype(jnp.bfloat16),
        down_proj[0],
        preferred_element_type=jnp.float32,
    )
    spare_out = jnp.einsum(
        "nsf,fd->nsd",
        jax.nn.silu(spare_part).astype(jnp.bfloat16),
        spare_down[0],
        preferred_element_type=jnp.float32,
    )
    terms = jnp.concatenate([main_out, spare_out], axis=1).astype(jnp.bfloat16)
    returned_parts = lax.all_to_all(terms, ("ep", "tp"), split_axis=0, concat_axis=0, tiled=True)
    returned = jnp.sum(
        returned_parts.reshape(experts, tp_lanes, slot_count, features).astype(jnp.float32), axis=1
    )
    slot_grid = slot_index.reshape(kept_rows, per_row)
    combine = jnp.sum(
        jnp.where(
            slot_grid[:, :, None] == jnp.arange(experts * slot_count)[None, None, :],
            route_gates[:, :, None],
            0.0,
        ),
        axis=1,
    )
    expert_sum = jnp.dot(
        combine,
        returned.reshape(experts * slot_count, features),
        precision=lax.Precision.HIGHEST,
        preferred_element_type=jnp.float32,
    )
    return (widened + expert_sum).astype(jnp.bfloat16)


def solution(mesh):
    return jax.shard_map(
        shards,
        mesh=mesh,
        in_specs=(
            P(("grp", "ep"), "tp"),
            P(("grp", "ep"), None),
            P(("grp", "ep", "tp"), None, None),
            P(("grp", "ep")),
            P(("grp", "ep", "tp"), None),
            P("tp", None),
            P(),
            P("ep", None, "tp"),
            P("ep", "tp", None),
            P(("grp", "ep", "tp"), None),
            P(("grp", "ep", "tp"), None),
            P("grp"),
            P("grp"),
        ),
        out_specs=P(("grp", "ep", "tp"), None),
        check_vma=False,
    )
```

profile of v0, /device:TPU:9, one launch (start us, length us, event | category | flops | bytes accessed | tf_op | source)
XLA Modules:
  0.0 260.6 jit_solution(7539846319061299161)
XLA Ops:
  6.5 0.7 all-gather.2.cloned.1.call-update
  7.3 0.0 reduce-scatter.2.cloned.1.call-start
  7.3 0.9 reshape.150
  8.2 0.1 copy.70
  8.3 0.1 iota_compare_fusion.4
  8.5 58.4 %all-gather.2.cloned.1.call-done = bf16[16,256,512]{2,1,0:T(8,128)(2,1)} async-done(((bf16[8,256,512]{2,1,0:T(8,128)(2,1)}), bf16[16,256,512]{2,1,0:T(8,128)(2,1)}) %all-gather.2.cloned.1.call-update) | async-done | bytes 4194320 | tf_op jit(solution)/shard_map/all_gather | solution.py:34
  66.8 2.6 %fusion.54 = (bf16[16,256,256]{2,1,0:T(8,128)(2,1)S(1)}, bf16[16,256,256]{2,1,0:T(8,128)(2,1)S(1)}) fusion(bf16[16,256,512]{2,1,0:T(8,128)(2,1)} %all-gather.2.cloned.1.call-done), kind=kLoop, calls=%fused_computation.73 | loop fusion | bytes 8388608 | tf_op jit(solution)/shard_map/slice | solution.py:37
  69.5 0.8 fusion.24
  70.4 0.7 fusion.57
  71.0 0.7 fusion.29
  71.7 0.2 copy.71
  71.9 12.8 %convolution_convert_fusion.1 = bf16[64,3584]{1,0:T(8,128)(2,1)} fusion(bf16[64,4096]{1,0:T(8,128)(2,1)S(1)} %bitcast.77, bf16[4096,3584]{1,0:T(8,128)(2,1)} %param.18), kind=kOutput, calls=%fused_computation.13 | convolution fusion | flops 1879277568 | bytes 30343168 | tf_op jit(solution)/shard_map/dot_general | solution.py:66
  84.8 0.1 copy.58
  84.9 0.1 eq.75
  85.7 0.1 copy.55
  85.7 0.1 reshape.164
  85.8 0.1 fusion.45
  85.9 0.1 reduce_window_sum.18
  86.0 0.1 reduce-window.4
  86.2 0.1 reduce
  86.3 0.6 fusion.50
  86.9 0.2 select_reduce_fusion.1
  87.1 0.6 fusion.47
  87.6 11.1 %reduce-scatter.2.cloned.1.call-done = bf16[32,3584]{1,0:T(8,128)(2,1)} async-done(((bf16[64,3584]{1,0:T(8,128)(2,1)}), bf16[32,3584]{1,0:T(8,128)(2,1)}) %reduce-scatter.2.cloned.1.call-update) | async-done | bytes 229392 | tf_op jit(solution)/shard_map/reduce_scatter | solution.py:65
  98.8 1.2 fusion.41
  100.0 1.1 fusion.43
  101.0 0.2 broadcast_in_dim.100
  101.3 0.6 reshape.155
  101.9 0.5 convolution_convert_fusion
  102.4 0.2 broadcast_in_dim.102
  102.7 68.0 %all_to_all.10 = bf16[16,24,3584]{2,1,0:T(8,128)(2,1)S(1)} all-to-all(bf16[16,24,3584]{2,1,0:T(8,128)(2,1)S(1)} %bitcast.75), channel_id=1, replica_groups=mesh['grp'=2,'ep'=8,'tp'=2] {'ep','tp'}, dimensions={0} | all-to-all | bytes 5505024 | tf_op jit(solution)/shard_map/all_to_all | solution.py:103
  170.6 0.4 fusion.55
  171.2 2.5 multiply_convert_fusion
  173.7 2.5 multiply_convert_fusion.1
  176.3 1.9 fusion.12
  178.3 1.9 fusion.9
  180.2 0.2 pad_maximum_fusion
  180.5 3.1 %copy.62 = bf16[16,24,3584]{2,1,0:T(8,128)(2,1)} copy(bf16[16,24,3584]{2,0,1:T(8,128)(2,1)S(1)} %pad_maximum_fusion) | data formatting | bytes 5505024 | tf_op jit(solution)/shard_map/concatenate | solution.py:122
  183.5 5.0 %all-to-all-start.1 = ((bf16[16,24,3584]{2,1,0:T(8,128)(2,1)}), bf16[16,24,3584]{2,1,0:T(8,128)(2,1)S(1)}, u32[]{:S(2)}, u32[]{:S(2)}) async-start(bf16[16,24,3584]{2,1,0:T(8,128)(2,1)} %copy.62), calls=%async_computation.2 | async-start | bytes 5505024 | tf_op jit(solution)/shard_map/all_to_all | solution.py:123
  188.5 0.1 reduce_sum.59
  188.6 0.1 reshape.153
  188.7 0.1 copy.59
  188.8 0.1 copy.57
  188.9 0.6 select_add_fusion
  189.5 0.1 select_reduce_fusion
  189.6 61.3 %all-to-all-done.1 = bf16[16,24,3584]{2,1,0:T(8,128)(2,1)S(1)} async-done(((bf16[16,24,3584]{2,1,0:T(8,128)(2,1)}), bf16[16,24,3584]{2,1,0:T(8,128)(2,1)S(1)}, u32[]{:S(2)}, u32[]{:S(2)}) %all-to-all-start.1) | async-done | bytes 2752544 | tf_op jit(solution)/shard_map/all_to_all | solution.py:123
  250.9 0.5 convert_reduce_fusion
  251.4 2.4 fusion.15
  (39 shorter events, 0.2 us)
Async XLA Ops:
  6.5 1.6 copy-start.2
  6.5 1.8 copy-start.6
  6.5 60.3 %all-gather.2.cloned.1.call-start = ((), (), s32[]{:S(2)}) async-start(), calls=%async_computation.3 | async-start | bytes 6291456 | tf_op jit(solution)/shard_map/all_gather | solution.py:34
  7.3 91.5 %reduce-scatter.2.cloned.1.call-start = ((), (), s32[]{:S(2)}) async-start(), calls=%async_computation.4 | async-start | bytes 688128 | tf_op jit(solution)/shard_map/reduce_scatter | solution.py:65
  71.9 12.9 %copy-start.3 = (s32[32,3]{0,1:T(4,128)S(1)}, s32[32,3]{0,1:T(4,128)}, u32[]{:S(2)}) copy-start(s32[32,3]{0,1:T(4,128)} %param.22) | copy-start | bytes 1156
  71.9 14.4 %copy-start.7 = (s32[8]{0:T(128)S(1)}, s32[8]{0:T(128)}, u32[]{:S(2)}) copy-start(s32[8]{0:T(128)} %param.25) | copy-start | bytes 100
  71.9 26.9 %copy-start = (bf16[32,3584]{1,0:T(8,128)(2,1)S(1)}, bf16[32,3584]{1,0:T(8,128)(2,1)}, u32[]{:S(2)}) copy-start(bf16[32,3584]{1,0:T(8,128)(2,1)} %param.17) | copy-start | bytes 688132
  71.9 28.1 %copy-start.4 = (f32[3584]{0:T(1024)S(1)}, f32[3584]{0:T(1024)}, u32[]{:S(2)}) copy-start(f32[3584]{0:T(1024)} %param.19) | copy-start | bytes 43012
  98.8 72.3 %slice-start = ((s8[9175040]{0:T(1024)(128)(4,1)}), s8[786432]{0:T(1024)(128)(4,1)S(1)}, s32[]{:S(2)}) async-start(s8[9175040]{0:T(1024)(128)(4,1)} %bitcast.81), calls=%async_computation.5 | async-start | bytes 1572864
  102.4 68.7 %slice-start.1 = ((s8[9175040]{0:T(1024)(128)(4,1)}), s8[4194304]{0:T(1024)(128)(4,1)S(1)}, s32[]{:S(2)}) async-start(s8[9175040]{0:T(1024)(128)(4,1)} %bitcast.81), calls=%async_computation.6 | async-start | bytes 8388608
  102.6 68.5 %slice-start.2 = ((s8[9175040]{0:T(1024)(128)(4,1)}), s8[4194304]{0:T(1024)(128)(4,1)S(1)}, s32[]{:S(2)}) async-start(s8[9175040]{0:T(1024)(128)(4,1)} %bitcast.81), calls=%async_computation.7 | async-start | bytes 8388608
  171.1 5.1 %slice-start.3 = ((s8[9175040]{0:T(1024)(128)(4,1)}), s8[786432]{0:T(1024)(128)(4,1)S(1)}, s32[]{:S(2)}) async-start(s8[9175040]{0:T(1024)(128)(4,1)} %bitcast.83), calls=%async_computation.8 | async-start | bytes 1572864
  171.2 5.1 %slice-start.4 = ((s8[9175040]{0:T(1024)(128)(4,1)}), s8[4194304]{0:T(1024)(128)(4,1)S(1)}, s32[]{:S(2)}) async-start(s8[9175040]{0:T(1024)(128)(4,1)} %bitcast.83), calls=%async_computation.9 | async-start | bytes 8388608
  173.7 2.6 slice-start.5
  183.5 5.9 %copy-start.5 = (f32[32,3]{0,1:T(4,128)S(1)}, f32[32,3]{0,1:T(4,128)}, u32[]{:S(2)}) copy-start(f32[32,3]{0,1:T(4,128)} %param.23) | copy-start | bytes 1156
  183.5 67.3 %all-to-all-start.1 = ((bf16[16,24,3584]{2,1,0:T(8,128)(2,1)}), bf16[16,24,3584]{2,1,0:T(8,128)(2,1)S(1)}, u32[]{:S(2)}, u32[]{:S(2)}) async-start(bf16[16,24,3584]{2,1,0:T(8,128)(2,1)} %copy.62), calls=%async_computation.2 | async-start | bytes 5505024 | tf_op jit(solution)/shard_map/all_to_all | solution.py:123
  189.6 61.8 %copy-start.1 = (bf16[32,3584]{1,0:T(8,128)(2,1)S(1)}, bf16[32,3584]{1,0:T(8,128)(2,1)}, u32[]{:S(2)}) copy-start(bf16[32,3584]{1,0:T(8,128)(2,1)} %reduce-scatter.2.cloned.1.call-done) | copy-start | bytes 688132
Sparse Core Ops, SparseCore 0:
  8.9 57.8 all-gather.1
  84.9 13.8 reduce-scatter.1
where the time goes:
time: 261 us
  waiting for transfers between devices  131 us (50%)
  blocking collectives  68 us (26%)
  matrix products  26.3 us (10%)
  between operations  14.5 us (6%)
  local copies, waits for them, and re-layouts  9.18 us (4%)
  other arithmetic  6.19 us (2%)
  starting transfers between devices  5.03 us (2%)
    all_to_all x1, blocking collectives, shards(): lax.all_to_all(copies, ('ep', 'tp'), split_axis=0, concat_axis=0, tiled=T...  68 us
    all_to_all x1, waiting for transfers between devices, shards(): lax.all_to_all(terms, ('ep', 'tp'), split_axis=0, concat_axis=0, tiled=True)  61.3 us
    all_gather x1, waiting for transfers between devices, shards(): block_rows = lax.all_gather(kv_cache, 'tp', axis=0, tiled=True)  58.4 us
    dot_general x1, matrix products, shards(): jnp.dot(attended, out_proj, preferred_element_type=jnp.float32)  12.8 us
    reduce_scatter x1, waiting for transfers between devices, shards(): lax.psum_scatter(jnp.dot(attended, out_proj, preferred_element_type=jnp.f...  11.1 us
  transfers between devices with their start and end apart: 3, of which 3 were waited for; matrix products, arithmetic and copies ran while one was open for 2% of the time, Pallas kernels for 0%

commit v1 on v0

--- a/solution.py
+++ b/solution.py
@@ -1,28 +1,245 @@
+import functools
 import math
 
 import jax
 import jax.numpy as jnp
 from jax import lax
+from jax.experimental import pallas as pl
+from jax.experimental.pallas import tpu as pltpu
 from jax.sharding import PartitionSpec as P
 
+MESH = pl.DeviceIdType.MESH
+TILE = 512
+
 EPSILON = 1e-06
 
 
-def shards(
-    queries,
-    draft_kv,
-    kv_cache,
+def attend_block(q_ref, out_ref, kv, draft, draft_at, lengths, first, head_dim, drafts):
+    requests, cached, _ = kv.shape
+    heads = q_ref.shape[1] // head_dim
+    factor = 1.0 / math.sqrt(head_dim)
+    pair = 2 * drafts
+    rows = heads * pair
+    spread = q_ref[...].astype(jnp.float32)
+    draft_keys = draft[draft_at, :, :head_dim]
+    draft_values = draft[draft_at, :, head_dim:]
+    mixed = []
+    for p in range(requests // 2):
+        here = jnp.concatenate(
+            [
+                spread[p * pair : (p + 1) * pair, h * head_dim : (h + 1) * head_dim]
+                for h in range(heads)
+            ],
+            0,
+        ).astype(jnp.bfloat16)
+        keys = kv[2 * p : 2 * p + 2, :, :head_dim].reshape(2 * cached, head_dim)
+        values = kv[2 * p : 2 * p + 2, :, head_dim:].reshape(2 * cached, head_dim)
+        scores = (
+            lax.dot_general(
+                here, keys, (((1,), (1,)), ((), ())), preferred_element_type=jnp.float32
+            )
+            * factor
+        )
+        row = lax.broadcasted_iota(jnp.int32, scores.shape, 0) % pair
+        column = lax.broadcasted_iota(jnp.int32, scores.shape, 1)
+        upper = row >= drafts
+        length = jnp.where(upper, lengths[first + 2 * p + 1] + cached, lengths[first + 2 * p])
+        begin = jnp.where(upper, cached, 0)
+        seen = (column >= begin) & (column < length)
+        late = (
+            lax.dot_general(
+                here, draft_keys, (((1,), (1,)), ((), ())), preferred_element_type=jnp.float32
+            )
+            * factor
+        )
+        late_row = lax.broadcasted_iota(jnp.int32, late.shape, 0) % pair
+        late_column = lax.broadcasted_iota(jnp.int32, late.shape, 1)
+        late_begin = jnp.where(late_row >= drafts, drafts, 0) + p * pair
+        late_seen = (late_column >= late_begin) & (late_column <= late_row + p * pair)
+        scores = jnp.where(seen, scores, -jnp.inf)
+        late = jnp.where(late_seen, late, -jnp.inf)
+        peak = jnp.maximum(
+            jnp.max(scores, axis=1, keepdims=True), jnp.max(late, axis=1, keepdims=True)
+        )
+        weights = jnp.exp(scores - peak)
+        late_weights = jnp.exp(late - peak)
+        totals = jnp.sum(weights, axis=1, keepdims=True) + jnp.sum(
+            late_weights, axis=1, keepdims=True
+        )
+        mixture = jnp.dot(
+            weights.astype(jnp.bfloat16), values, preferred_element_type=jnp.float32
+        ) + jnp.dot(
+            late_weights.astype(jnp.bfloat16), draft_values, preferred_element_type=jnp.float32
+        )
+        mixed.append(mixture / totals)
+    for h in range(heads):
+        out_ref[:, h * head_dim : (h + 1) * head_dim] = jnp.concatenate(
+            [part[h * pair : (h + 1) * pair] for part in mixed], 0
+        ).astype(jnp.bfloat16)
+
+
+def attend_kernel(
+    q,
+    draft,
+    kv,
     lengths,
     residual,
-    out_proj,
-    norm_gain,
-    up_proj,
-    down_proj,
-    routes,
-    route_gates,
-    lost_device,
-    spare_table,
+    w,
+    gain,
+    hidden_out,
+    normed_out,
+    q_own,
+    q_in,
+    kv_v,
+    w_v,
+    att_own,
+    att_out,
+    att_in,
+    total,
+    proj_out,
+    proj_in,
+    local_sem,
+    w_sem,
+    q_sem,
+    att_sem,
+    send_sem,
+    recv_sem,
 ):
+    me = lax.axis_index("tp")
+    peer = 1 - me
+    head_dim = kv.shape[2] // 2
+    requests = kv.shape[0]
+    drafts = q.shape[1] // requests
+    tiles = w_v.shape[0]
+    q_copy = pltpu.make_async_copy(q.at[me], q_own, local_sem.at[0])
+    kv_copy = pltpu.make_async_copy(kv, kv_v, local_sem.at[1])
+    q_copy.start()
+    kv_copy.start()
+
+    def w_copy(n):
+        return pltpu.make_async_copy(
+            w.at[:, pl.ds(pl.multiple_of(n * TILE, TILE), TILE)], w_v.at[n], w_sem.at[n]
+        )
+
+    for n in range(tiles):
+        w_copy(n).start()
+    barrier = pltpu.get_barrier_semaphore()
+    pl.semaphore_signal(barrier, inc=1, device_id={"tp": peer}, device_id_type=MESH)
+    pl.semaphore_wait(barrier, 1)
+
+    def remote(source, target, send, recv):
+        return pltpu.make_async_remote_copy(
+            src_ref=source,
+            dst_ref=target,
+            send_sem=send,
+            recv_sem=recv,
+            device_id={"tp": peer},
+            device_id_type=MESH,
+        )
+
+    ask = remote(q.at[peer], q_in, q_sem.at[0], q_sem.at[1])
+    ask.start()
+    q_copy.wait()
+    kv_copy.wait()
+    first = me * requests
+    attend_block(q_own, att_own, kv_v, draft, me, lengths, first, head_dim, drafts)
+    ask.wait()
+    attend_block(q_in, att_out, kv_v, draft, me, lengths, first, head_dim, drafts)
+    answer = remote(att_out, att_in, att_sem.at[0], att_sem.at[1])
+    answer.start()
+
+    def own_part(n, carry):
+        w_copy(n).wait()
+        total[n] = jnp.dot(att_own[...], w_v[n], preferred_element_type=jnp.float32)
+        return carry
+
+    lax.fori_loop(0, tiles, own_part, 0)
+    answer.wait()
+
+    def give(n):
+        return remote(proj_out.at[n], proj_in.at[n], send_sem.at[n], recv_sem.at[n])
+
+    def peer_part(n, carry):
+        proj_out[n] = jnp.dot(
+            att_in[...], w_v[n], preferred_element_type=jnp.float32
+        ).astype(jnp.bfloat16)
+        give(n).start()
+        return carry
+
+    lax.fori_loop(0, tiles, peer_part, 0)
+    squares = jnp.zeros((residual.shape[0], 1), jnp.float32)
+    for n in range(tiles):
+        give(n).wait()
+        lanes = slice(n * TILE, (n + 1) * TILE)
+        hidden = (
+            residual[:, lanes].astype(jnp.float32)
+            + total[n]
+            + proj_in[n].astype(jnp.float32)
+        ).astype(jnp.bfloat16)
+        hidden_out[:, lanes] = hidden
+        widened = hidden.astype(jnp.float32)
+        squares += jnp.sum(widened * widened, axis=1, keepdims=True)
+    scale = lax.rsqrt(squares / residual.shape[1] + EPSILON)
+    for n in range(tiles):
+        lanes = slice(n * TILE, (n + 1) * TILE)
+        normed_out[:, lanes] = (
+            hidden_out[:, lanes].astype(jnp.float32) * scale * gain[:, lanes]
+        ).astype(jnp.bfloat16)
+
+
+def attend_paired(queries, draft_kv, kv_cache, lengths, residual, out_proj, norm_gain):
+    rows, features = residual.shape
+    width = queries.shape[1]
+    tiles = features // TILE
+    vmem = pl.BlockSpec(memory_space=pltpu.VMEM)
+    hbm = pl.BlockSpec(memory_space=pl.ANY)
+    half = jax.ShapeDtypeStruct((rows, features), jnp.bfloat16)
+    return pl.pallas_call(
+        attend_kernel,
+        out_shape=(half, half),
+        in_specs=[
+            hbm,
+            vmem,
+            hbm,
+            pl.BlockSpec(memory_space=pltpu.SMEM),
+            vmem,
+            hbm,
+            vmem,
+        ],
+        out_specs=(vmem, vmem),
+        scratch_shapes=[
+            pltpu.VMEM((rows, width), jnp.bfloat16),
+            pltpu.VMEM((rows, width), jnp.bfloat16),
+            pltpu.VMEM(kv_cache.shape, jnp.bfloat16),
+            pltpu.VMEM((tiles, width, TILE), jnp.bfloat16),
+            pltpu.VMEM((rows, width), jnp.bfloat16),
+            pltpu.VMEM((rows, width), jnp.bfloat16),
+            pltpu.VMEM((rows, width), jnp.bfloat16),
+            pltpu.VMEM((tiles, rows, TILE), jnp.float32),
+            pltpu.VMEM((tiles, rows, TILE), jnp.bfloat16),
+            pltpu.VMEM((tiles, rows, TILE), jnp.bfloat16),
+            pltpu.SemaphoreType.DMA((2,)),
+            pltpu.SemaphoreType.DMA((tiles,)),
+            pltpu.SemaphoreType.DMA((2,)),
+            pltpu.SemaphoreType.DMA((2,)),
+            pltpu.SemaphoreType.DMA((tiles,)),
+            pltpu.SemaphoreType.DMA((tiles,)),
+        ],
+        compiler_params=pltpu.CompilerParams(
+            collective_id=0, has_side_effects=True, vmem_limit_bytes=48 * 1024 * 1024
+        ),
+    )(
+        queries.reshape(2, rows, width),
+        draft_kv.reshape(2, rows, draft_kv.shape[1]),
+        kv_cache,
+        lengths,
+        residual,
+        out_proj,
+        norm_gain.reshape(1, features),
+    )
+
+
+def attend_general(queries, draft_kv, kv_cache, lengths, residual, out_proj, norm_gain):
     requests = lengths.shape[0]
     drafts = draft_kv.shape[0] // requests
     head_dim = draft_kv.shape[1] // 2
@@ -75,6 +292,31 @@
         * lax.rsqrt(jnp.mean(widened * widened, axis=-1, keepdims=True) + EPSILON)
         * norm_gain
     ).astype(jnp.bfloat16)
+    return hidden, normed
+
+
+def shards(
+    queries,
+    draft_kv,
+    kv_cache,
+    lengths,
+    residual,
+    out_proj,
+    norm_gain,
+    up_proj,
+    down_proj,
+    routes,
+    route_gates,
+    lost_device,
+    spare_table,
+):
+    kept_rows, features = residual.shape
+    paired = lax.axis_size("tp") == 2 and kv_cache.shape[0] % 8 == 0
+    attend = attend_paired if paired else attend_general
+    hidden, normed = attend(
+        queries, draft_kv, kv_cache, lengths, residual, out_proj, norm_gain
+    )
+    widened = hidden.astype(jnp.float32)
     experts = lax.axis_size("ep")
     tp_lanes = lax.axis_size("tp")
     per_row = routes.shape[1]

time: 261 us -> 190 us (0.73)
  waiting for transfers between devices: 131 us -> 61.2 us
  Pallas kernels: 0 us -> 24.2 us
  matrix products: 26.3 us -> 11.9 us
  between operations: 14.5 us -> 0.93 us
  blocking collectives: 68 us -> 70.7 us
  local copies, waits for them, and re-layouts: 9.18 us -> 11.8 us
    all_gather x1 -> x0, waiting for transfers between devices: 58.4 us -> none  [shards(): block_rows = lax.all_gather(kv_cache, 'tp', axis=0, tiled=True)]
    pallas_call x0 -> x1, Pallas kernels: none -> 24.2 us  [attend_paired(): pl.pallas_call(attend_kernel, out_shape=(half, half), in_specs=[hbm, vmem...]
    dot_general x3 -> x0, matrix products: 14.4 us -> none  [the longest x1 12.8 us: shards(): jnp.dot(attended, out_proj, preferred_element_type=jnp.float32)]
    reduce_scatter x1 -> x0, waiting for transfers between devices: 11.1 us -> none  [shards(): lax.psum_scatter(jnp.dot(attended, out_proj, preferred_element_type=jnp.f...]
    unnamed x31 -> x25, local copies, waits for them, and re-layouts: 0.45 us -> 5.86 us
    all_to_all x1, blocking collectives: 68 us -> 70.7 us  [shards(): lax.all_to_all(copies, ('ep', 'tp'), split_axis=0, concat_axis=0, tiled=T...]
    slice x2 -> x0, local copies, waits for them, and re-layouts: 2.67 us -> none  [the longest x1 2.65 us: shards(): block_rows[:, :, :head_dim]]
  transfers between devices with their start and end apart: 3 -> 1, of which waited for: 3 -> 1; matrix products, arithmetic and copies ran while one was open for 2% -> 1% of each run, Pallas kernels for 0% -> 0%
where the time goes in v1:
time: 190 us
  blocking collectives  70.7 us (37%)
  waiting for transfers between devices  61.2 us (32%)
  Pallas kernels  24.2 us (13%)
  matrix products  11.9 us (6%)
  local copies, waits for them, and re-layouts  11.8 us (6%)
  starting transfers between devices  4.99 us (3%)
  other arithmetic  4.19 us (2%)
    all_to_all x1, blocking collectives, shards(): lax.all_to_all(copies, ('ep', 'tp'), split_axis=0, concat_axis=0, tiled=T...  70.7 us
    all_to_all x1, waiting for transfers between devices, shards(): lax.all_to_all(terms, ('ep', 'tp'), split_axis=0, concat_axis=0, tiled=True)  61.2 us
    pallas_call x1, Pallas kernels, attend_paired(): pl.pallas_call(attend_kernel, out_shape=(half, half), in_specs=[hbm, vmem...  24.2 us
    unnamed x25, local copies, waits for them, and re-layouts  5.86 us
    all_to_all x1, starting transfers between devices, shards(): lax.all_to_all(terms, ('ep', 'tp'), split_axis=0, concat_axis=0, tiled=True)  4.99 us
  transfers between devices with their start and end apart: 1, of which 1 were waited for; matrix products, arithmetic and copies ran while one was open for 1% of the time, Pallas kernels for 0%

profile of v1, /device:TPU:9, one launch (start us, length us, event | category | flops | bytes accessed | tf_op | source)
XLA Modules:
  0.0 189.9 jit_solution(9067866928537867299)
XLA Ops:
  0.0 0.8 copy.58
  0.8 0.1 eq.75
  0.9 0.1 fusion.26
  1.0 0.1 reduce_window_sum.18
  1.1 0.2 select_reduce_fusion.1
  1.9 0.7 compare_convert_fusion
  2.6 0.1 copy.55
  2.7 0.1 reshape.95
  2.8 0.1 reduce-window.4
  2.9 0.1 reduce
  3.0 0.7 reshape.85.gain
  3.8 0.0 copy-start
  3.8 1.6 copy-done
  5.4 1.0 copy-done.1
  6.4 0.9 copy-done.2
  7.4 0.8 copy-done.3
  8.2 0.7 copy-done.4
  8.9 24.2 %shard_map.127 = (bf16[32,3584]{1,0:T(8,128)(2,1)S(1)}, bf16[32,3584]{1,0:T(8,128)(2,1)S(1)}) custom-call(bf16[2,32,4096]{2,1,0:T(8,128)(2,1)S(1)} %bitcast.38, bf16[2,32,512]{2,1,0:T(8,128)(2,1)S(1)} %bitcast.39, bf16[8,256,512]{2,1,0:T(8,128)(2,1)S(1)} %copy-done, s32[16]{0:T(128)S(1)} %copy-done.4, bf16[32,3584]{1,0:T(8,128)(2,1)S(1)} %copy-done.2, ...), custom_call_target="tpu_custom_call" | custom-call | tf_op jit(solution)/shard_map/pallas_call | solution.py:197
  33.1 0.0 copy-start.8
  33.1 0.2 broadcast_in_dim.42
  33.3 0.6 reshape.88
  34.0 0.7 fusion.31
  34.7 0.7 fusion.28
  35.3 0.5 convolution_convert_fusion
  35.8 0.2 broadcast_in_dim.44
  36.1 0.0 copy-start.7
  36.1 70.7 %all_to_all.10 = bf16[16,24,3584]{2,1,0:T(8,128)(2,1)S(1)} all-to-all(bf16[16,24,3584]{2,1,0:T(8,128)(2,1)S(1)} %bitcast.41), channel_id=1, replica_groups=mesh['grp'=2,'ep'=8,'tp'=2] {'ep','tp'}, dimensions={0} | all-to-all | bytes 5505024 | tf_op jit(solution)/shard_map/all_to_all | solution.py:345
  106.7 0.4 fusion.32
  107.2 0.0 slice-start
  107.2 0.0 slice-start.1
  107.2 2.5 %multiply_convert_fusion = bf16[16,12,1280]{2,0,1:T(8,128)(2,1)S(1)} fusion(bf16[1,3584,1280]{2,1,0:T(8,128)(2,1)S(1)} %copy-done.7, bf16[16,12,3584]{2,1,0:T(8,128)(2,1)S(1)} %get-tuple-element.10), kind=kOutput, calls=%fused_computation.17 | convolution fusion | flops 1762836480 | bytes 11042816 | tf_op jit(solution)/shard_map/nsd,df->nsf/dot_general | solution.py:349
  109.8 0.0 slice-start.2
  109.8 2.5 %multiply_convert_fusion.1 = bf16[16,12,1280]{2,0,1:T(8,128)(2,1)S(1)} fusion(bf16[1,3584,1280]{2,1,0:T(8,128)(2,1)S(1)} %copy-done.7, bf16[16,12,3584]{2,1,0:T(8,128)(2,1)S(1)} %get-tuple-element.9), kind=kOutput, calls=%fused_computation.18 | convolution fusion | flops 1762836480 | bytes 11042816 | tf_op jit(solution)/shard_map/nsd,df->nsf/dot_general | solution.py:346
  112.4 1.9 %fusion.11 = bf16[16,12,3584]{2,0,1:T(8,128)(2,1)S(1)} fusion(bf16[16,12,1280]{2,0,1:T(8,128)(2,1)S(1)} %multiply_convert_fusion, bf16[1,1280,3584]{2,1,0:T(8,128)(2,1)S(1)} %bitcast.44), kind=kOutput, calls=%fused_computation.10 | convolution fusion | flops 1762295808 | bytes 11042816 | tf_op jit(solution)/shard_map/nsf,fd->nsd/dot_general | solution.py:358
  114.3 1.9 %fusion.8 = bf16[16,12,3584]{2,0,1:T(8,128)(2,1)S(1)} fusion(bf16[16,12,1280]{2,0,1:T(8,128)(2,1)S(1)} %multiply_convert_fusion.1, bf16[1,1280,3584]{2,1,0:T(8,128)(2,1)S(1)} %bitcast.44), kind=kOutput, calls=%fused_computation.9 | convolution fusion | flops 1762295808 | bytes 11042816 | tf_op jit(solution)/shard_map/nsf,fd->nsd/dot_general | solution.py:352
  116.3 0.2 pad_maximum_fusion
  116.5 3.1 %copy.62 = bf16[16,24,3584]{2,1,0:T(8,128)(2,1)} copy(bf16[16,24,3584]{2,0,1:T(8,128)(2,1)S(1)} %pad_maximum_fusion) | data formatting | bytes 5505024 | tf_op jit(solution)/shard_map/concatenate | solution.py:364
  119.6 5.0 %all-to-all-start.1 = ((bf16[16,24,3584]{2,1,0:T(8,128)(2,1)}), bf16[16,24,3584]{2,1,0:T(8,128)(2,1)S(1)}, u32[]{:S(2)}, u32[]{:S(2)}) async-start(bf16[16,24,3584]{2,1,0:T(8,128)(2,1)} %copy.62), calls=%async_computation.1 | async-start | bytes 5505024 | tf_op jit(solution)/shard_map/all_to_all | solution.py:365
  124.6 0.1 reduce_sum.40
  124.7 0.1 reshape.86
  124.8 0.1 copy.59
  124.9 0.1 copy.57
  125.0 0.7 select_add_fusion
  125.7 0.0 copy-done.6
  125.7 0.1 select_reduce_fusion
  125.8 61.2 %all-to-all-done.1 = bf16[16,24,3584]{2,1,0:T(8,128)(2,1)S(1)} async-done(((bf16[16,24,3584]{2,1,0:T(8,128)(2,1)}), bf16[16,24,3584]{2,1,0:T(8,128)(2,1)S(1)}, u32[]{:S(2)}, u32[]{:S(2)}) %all-to-all-start.1) | async-done | bytes 2752544 | tf_op jit(solution)/shard_map/all_to_all | solution.py:365
  186.9 0.5 convert_reduce_fusion
  187.4 2.4 %fusion.14 = bf16[32,3584]{1,0:T(8,128)(2,1)} fusion(f32[32,192]{1,0:T(8,128)S(1)} %select_reduce_fusion, f32[192,3584]{1,0:T(8,128)S(1)} %bitcast.40, bf16[32,3584]{1,0:T(8,128)(2,1)S(1)} %get-tuple-element.7), kind=kOutput, calls=%fused_computation.13 | convolution fusion | flops 264585216 | bytes 3235840 | tf_op jit(solution)/shard_map/dot_general | solution.py:378
  (13 shorter events, 0.0 us)
Async XLA Ops:
  3.8 1.6 copy-start
  5.4 1.0 copy-start.1
  6.4 0.9 copy-start.2
  7.4 0.8 copy-start.3
  8.2 0.7 copy-start.4
  33.1 0.9 copy-start.8
  36.1 71.1 %copy-start.7 = (bf16[1,3584,1280]{2,1,0:T(8,128)(2,1)S(1)}, bf16[1,3584,1280]{2,1,0:T(8,128)(2,1)}, u32[]{:S(2)}) copy-start(bf16[1,3584,1280]{2,1,0:T(8,128)(2,1)} %param.20) | copy-start | bytes 27525124
  107.2 5.1 %slice-start = ((s8[9175040]{0:T(1024)(128)(4,1)}), s8[4194304]{0:T(1024)(128)(4,1)S(1)}, s32[]{:S(2)}) async-start(s8[9175040]{0:T(1024)(128)(4,1)} %bitcast.43), calls=%async_computation.2 | async-start | bytes 8388608
  107.2 5.1 %slice-start.1 = ((s8[9175040]{0:T(1024)(128)(4,1)}), s8[4194304]{0:T(1024)(128)(4,1)S(1)}, s32[]{:S(2)}) async-start(s8[9175040]{0:T(1024)(128)(4,1)} %bitcast.43), calls=%async_computation.3 | async-start | bytes 8388608
  109.8 2.6 %slice-start.2 = ((s8[9175040]{0:T(1024)(128)(4,1)}), s8[786432]{0:T(1024)(128)(4,1)S(1)}, s32[]{:S(2)}) async-start(s8[9175040]{0:T(1024)(128)(4,1)} %bitcast.43), calls=%async_computation.4 | async-start | bytes 1572864
  119.6 5.4 %copy-start.5 = (s32[32,3]{0,1:T(4,128)S(1)}, s32[32,3]{0,1:T(4,128)}, u32[]{:S(2)}) copy-start(s32[32,3]{0,1:T(4,128)} %param.22) | copy-start | bytes 1156
  119.6 6.1 %copy-start.6 = (f32[32,3]{0,1:T(4,128)S(1)}, f32[32,3]{0,1:T(4,128)}, u32[]{:S(2)}) copy-start(f32[32,3]{0,1:T(4,128)} %param.23) | copy-start | bytes 1156
  119.6 67.3 %all-to-all-start.1 = ((bf16[16,24,3584]{2,1,0:T(8,128)(2,1)}), bf16[16,24,3584]{2,1,0:T(8,128)(2,1)S(1)}, u32[]{:S(2)}, u32[]{:S(2)}) async-start(bf16[16,24,3584]{2,1,0:T(8,128)(2,1)} %copy.62), calls=%async_computation.1 | async-start | bytes 5505024 | tf_op jit(solution)/shard_map/all_to_all | solution.py:365

commit v2 on v1

--- a/solution.py
+++ b/solution.py
@@ -226,7 +226,7 @@
             pltpu.SemaphoreType.DMA((tiles,)),
         ],
         compiler_params=pltpu.CompilerParams(
-            collective_id=0, has_side_effects=True, vmem_limit_bytes=48 * 1024 * 1024
+            collective_id=0, has_side_effects=True, vmem_limit_bytes=60 * 1024 * 1024
         ),
     )(
         queries.reshape(2, rows, width),
@@ -237,6 +237,379 @@
         out_proj,
         norm_gain.reshape(1, features),
     )
+
+
+def expert_kernel(
+    hidden,
+    normed,
+    gate_code,
+    up,
+    down,
+    out,
+    xa,
+    xb,
+    up_v,
+    down_v,
+    act,
+    ya,
+    yb,
+    core_a,
+    core_b,
+    side_b,
+    side_in_b,
+    chain_a,
+    chain_b,
+    below_a,
+    below_b,
+    above_a,
+    above_b,
+    last_a,
+    last_b,
+    last_in_a,
+    weight_sem,
+    x_send,
+    x_recv,
+    core_send,
+    core_recv,
+    side_send,
+    side_recv,
+    chain_send,
+    below_recv,
+    above_recv,
+    last_sem,
+):
+    ep = lax.axis_index("ep")
+    tx = lax.axis_index("tp")
+    z = ep // 2
+    c = ep % 2
+    other = 1 - c
+    peer = 1 - tx
+    levels, _, _, rows, width_a = xa.shape
+    features = normed.shape[1]
+    width_b = features - width_a
+    inner = up.shape[2]
+    up_copy = pltpu.make_async_copy(up.at[0], up_v, weight_sem.at[0])
+    down_copy = pltpu.make_async_copy(down.at[0], down_v, weight_sem.at[1])
+    up_copy.start()
+    down_copy.start()
+    has_up = z < levels - 1
+    has_down = z > 0
+    places = (
+        {"ep": ep + 2},
+        {"ep": ep - 2},
+        {"tp": peer},
+        {"ep": z * 2 + other},
+    )
+    conditions = (has_up, has_down, None, None)
+
+    def when(condition, action):
+        if condition is None:
+            action()
+        else:
+            pl.when(condition)(action)
+
+    xa[z, c, tx] = normed[:, :width_a]
+    xb[z, c, tx, :, :width_b] = normed[:, width_a:]
+    xb[z, c, tx, :, width_b:] = gate_code[...]
+    barrier = pltpu.get_barrier_semaphore()
+    for place, condition in zip(places, conditions):
+        when(
+            condition,
+            functools.partial(
+                pl.semaphore_signal, barrier, inc=1, device_id=place, device_id_type=MESH
+            ),
+        )
+    neighbours = 2 + (z + levels - 1) // levels + (2 * levels - 2 - z) // levels
+    pl.semaphore_wait(barrier, neighbours)
+
+    pending = []
+
+    def both(first, second):
+        return first if second is None else (second if first is None else first & second)
+
+    def start(condition, build):
+        when(condition, lambda: build().start())
+        pending.append((condition, build))
+
+    def remote(source, target, send, recv, way):
+        return pltpu.make_async_remote_copy(
+            src_ref=source,
+            dst_ref=target,
+            send_sem=send,
+            recv_sem=recv,
+            device_id=places[way],
+            device_id_type=MESH,
+        )
+
+    blocks = (xa, xb)
+
+    def block(part, way, zb, xt):
+        return remote(
+            blocks[part].at[zb, c, xt],
+            blocks[part].at[zb, c, xt],
+            x_send.at[part, way, zb, xt],
+            x_recv.at[part, zb, c, xt],
+            way,
+        )
+
+    def pass_on(part, ways, zb, xt, condition=None):
+        for way in ways:
+            start(
+                both(condition, conditions[way]),
+                functools.partial(block, part, way, zb, xt),
+            )
+
+    def landed(part, zb, cb, xt):
+        pltpu.make_async_remote_copy(
+            src_ref=blocks[part].at[zb, cb, xt],
+            dst_ref=blocks[part].at[zb, cb, xt],
+            send_sem=x_send.at[part, 2, zb, xt],
+            recv_sem=x_recv.at[part, zb, cb, xt],
+            device_id=places[2],
+            device_id_type=MESH,
+        ).wait_recv()
+
+    def phase(d):
+        if d == 0:
+            pass_on(0, (2, 0, 1), z, tx)
+            pass_on(1, (0, 1, 2), z, tx)
+            pass_on(0, (3,), z, tx)
+            pass_on(1, (3,), z, tx)
+            landed(0, z, c, peer)
+            pass_on(0, (0, 1, 3), z, peer)
+            landed(1, z, c, peer)
+            pass_on(1, (3,), z, peer)
+            return
+        sides = ((z - d, z >= d, 0), (z + d, z + d < levels, 1))
+        for part, xt in ((0, tx), (1, tx), (0, peer)):
+            for zb, valid, way in sides:
+                when(valid, functools.partial(landed, part, zb, c, xt))
+                pass_on(part, (way, 2, 3) if part == 1 else (way, 3), zb, xt, valid)
+        for zb, valid, way in sides:
+            when(valid, functools.partial(landed, 1, zb, c, peer))
+            pass_on(1, (3,), zb, peer, valid)
+
+    tile = 256
+    wide = 512
+
+    def feed(zk):
+        for part in (0, 1):
+            for xt in (0, 1):
+                landed(part, zk, other, xt)
+        count = 4 * rows
+        code = xb[zk, :, :, :, width_b:].reshape(count, 128).astype(jnp.float32)
+        lane = lax.broadcasted_iota(jnp.int32, code.shape, 1) % 64
+        gate = jnp.sum(jnp.where(lane == ep, code, 0.0), axis=1, keepdims=True)
+
+        def rise(n, carry):
+            lanes = pl.ds(pl.multiple_of(n * tile, tile), tile)
+            value = jnp.dot(
+                xa[zk].reshape(count, width_a),
+                up_v[:width_a, lanes],
+                preferred_element_type=jnp.float32,
+            ) + jnp.dot(
+                xb[zk, :, :, :, :width_b].reshape(count, width_b),
+                up_v[width_a:, lanes],
+                preferred_element_type=jnp.float32,
+            )
+            act[:, lanes] = (value / (1.0 + jnp.exp(-value))).astype(jnp.bfloat16)
+            return carry
+
+        lax.fori_loop(0, inner // tile, rise, 0)
+
+        def fall(target, offset, n, carry):
+            value = jnp.dot(
+                act[...],
+                down_v[:, pl.ds(pl.multiple_of(offset + n * wide, wide), wide)],
+                preferred_element_type=jnp.float32,
+            )
+            target[zk, :, :, :, pl.ds(pl.multiple_of(n * wide, wide), wide)] = (
+                (value * gate).astype(jnp.bfloat16).reshape(2, 2, rows, wide)
+            )
+            return carry
+
+        lax.fori_loop(0, width_a // wide, functools.partial(fall, ya, 0), 0)
+        lax.fori_loop(0, width_b // wide, functools.partial(fall, yb, width_a), 0)
+
+    def core_copy(part, zk):
+        source, target = ((ya, core_a), (yb, core_b))[part]
+        return remote(
+            source.at[zk, other],
+            target.at[zk],
+            core_send.at[part, zk],
+            core_recv.at[part, zk],
+            3,
+        )
+
+    def side_copy(zk):
+        return remote(side_b.at[zk], side_in_b.at[zk], side_send.at[zk], side_recv.at[zk], 2)
+
+    f32 = jnp.float32
+
+    def settle(zk):
+        core_copy(1, zk).wait_recv()
+        side_b[zk] = (yb[zk, c, peer].astype(f32) + core_b[zk, peer].astype(f32)).astype(
+            jnp.bfloat16
+        )
+        start(None, functools.partial(side_copy, zk))
+        core_copy(0, zk).wait_recv()
+
+    order = (z, z + 1 - 2 * (z % 2), (z + 2) % 4, 3 - z)
+    for k in range(levels):
+        phase(k)
+        if k == 0:
+            up_copy.wait()
+            down_copy.wait()
+        feed(order[k])
+        for part in (1, 0):
+            start(None, functools.partial(core_copy, part, order[k]))
+        if k > 0:
+            settle(order[k - 1])
+    settle(order[levels - 1])
+
+    arrivals = ((below_a, below_b, below_recv), (above_a, above_b, above_recv))
+
+    def chain_copy(part, way, zb):
+        return remote(
+            (chain_a, chain_b)[part].at[zb],
+            arrivals[way][part].at[zb],
+            chain_send.at[part, zb],
+            arrivals[way][2].at[part, zb],
+            way,
+        )
+
+    def own_a(zb):
+        return ya[zb, c].astype(f32) + core_a[zb].astype(f32)
+
+    def own_b(zb):
+        side_copy(zb).wait_recv()
+        return (
+            yb[zb, c, tx].astype(f32) + core_b[zb, tx].astype(f32) + side_in_b[zb].astype(f32)
+        )
+
+    for d in range(levels - 1, 0, -1):
+        for way, zb, valid, joined in (
+            (0, z + d, z + d < levels, has_down),
+            (1, z - d, z >= d, has_up),
+        ):
+
+            def hop(way=way, zb=zb, joined=joined):
+                chain_a[zb] = own_a(zb).astype(jnp.bfloat16)
+                chain_b[zb] = own_b(zb).astype(jnp.bfloat16)
+
+                def join():
+                    for part, held in ((0, chain_a), (1, chain_b)):
+                        chain_copy(part, way, zb).wait_recv()
+                        held[zb] = (
+                            held[zb].astype(f32) + arrivals[way][part][zb].astype(f32)
+                        ).astype(jnp.bfloat16)
+
+                pl.when(joined)(join)
+
+            pl.when(valid)(hop)
+            for part in (0, 1):
+                start(valid, functools.partial(chain_copy, part, way, zb))
+
+    last_a[...] = own_a(z)
+    side = own_b(z)
+    last_b[...] = side + hidden[:, width_a:].astype(f32)
+
+    def gather_a(way):
+        chain_copy(0, way, z).wait_recv()
+        last_a[...] += arrivals[way][0][z].astype(f32)
+
+    pl.when(has_down)(functools.partial(gather_a, 0))
+    pl.when(has_up)(functools.partial(gather_a, 1))
+    chain_a[z] = last_a[...].astype(jnp.bfloat16)
+
+    def last_copy():
+        return remote(chain_a.at[z, peer], last_in_a, last_sem.at[0], last_sem.at[1], 2)
+
+    start(None, last_copy)
+
+    def gather_b(way):
+        chain_copy(1, way, z).wait_recv()
+        last_b[...] += arrivals[way][1][z].astype(f32)
+
+    pl.when(has_down)(functools.partial(gather_b, 0))
+    pl.when(has_up)(functools.partial(gather_b, 1))
+    out[:, width_a:] = last_b[...].astype(jnp.bfloat16)
+    last_copy().wait_recv()
+    out[:, :width_a] = (
+        hidden[:, :width_a].astype(f32) + last_a[tx] + last_in_a[...].astype(f32)
+    ).astype(jnp.bfloat16)
+    for condition, build in pending:
+        when(condition, lambda: build().wait_send())
+
+
+def experts_paired(hidden, normed, gate_code, up_proj, down_proj):
+    rows, features = hidden.shape
+    inner = up_proj.shape[2]
+    levels = lax.axis_size("ep") // 2
+    width_a = 1536
+    width_b = features - width_a
+    vmem = pl.BlockSpec(memory_space=pltpu.VMEM)
+    hbm = pl.BlockSpec(memory_space=pl.ANY)
+    dma = pltpu.SemaphoreType.DMA
+
+    def held(*shape, dtype=jnp.bfloat16):
+        return pltpu.VMEM(shape, dtype)
+
+    return pl.pallas_call(
+        expert_kernel,
+        out_shape=jax.ShapeDtypeStruct((rows, features), jnp.bfloat16),
+        in_specs=[vmem, vmem, vmem, hbm, hbm],
+        out_specs=vmem,
+        scratch_shapes=[
+            held(levels, 2, 2, rows, width_a),
+            held(levels, 2, 2, rows, width_b + 128),
+            held(features, inner),
+            held(inner, features),
+            held(4 * rows, inner),
+            held(levels, 2, 2, rows, width_a),
+            held(levels, 2, 2, rows, width_b),
+            held(levels, 2, rows, width_a),
+            held(levels, 2, rows, width_b),
+            held(levels, rows, width_b),
+            held(levels, rows, width_b),
+            held(levels, 2, rows, width_a),
+            held(levels, rows, width_b),
+            held(levels, 2, rows, width_a),
+            held(levels, rows, width_b),
+            held(levels, 2, rows, width_a),
+            held(levels, rows, width_b),
+            held(2, rows, width_a, dtype=jnp.float32),
+            held(rows, width_b, dtype=jnp.float32),
+            held(rows, width_a),
+            dma((2,)),
+            dma((2, 4, levels, 2)),
+            dma((2, levels, 2, 2)),
+            dma((2, levels)),
+            dma((2, levels)),
+            dma((levels,)),
+            dma((levels,)),
+            dma((2, levels)),
+            dma((2, levels)),
+            dma((2, levels)),
+            dma((2,)),
+        ],
+        compiler_params=pltpu.CompilerParams(
+            collective_id=1, has_side_effects=True, vmem_limit_bytes=60 * 1024 * 1024
+        ),
+    )(hidden, normed, gate_code, up_proj, down_proj)
+
+
+def code_gates(routes, route_gates, lost_device, spare_table):
+    experts = lax.axis_size("ep")
+    lost_id = lost_device[0]
+    spare_id = jnp.sum(jnp.where(jnp.arange(experts) == lost_id, spare_table, 0))
+    target = jnp.where(routes == lost_id, spare_id, routes)
+    lane = jnp.arange(128)[None, None, :]
+    gates = jnp.sum(
+        jnp.where(target[:, :, None] == lane % 64, route_gates[:, :, None], 0.0), axis=1
+    )
+    high = lax.reduce_precision(gates, 8, 7)
+    return jnp.where(lane[0] < 64, high, gates - high).astype(jnp.bfloat16)
 
 
 def attend_general(queries, draft_kv, kv_cache, lengths, residual, out_proj, norm_gain):
@@ -317,6 +690,9 @@
         queries, draft_kv, kv_cache, lengths, residual, out_proj, norm_gain
     )
     widened = hidden.astype(jnp.float32)
+    if paired and lax.axis_size("ep") == 8 and kept_rows % 16 == 0:
+        gate_code = code_gates(routes, route_gates, lost_device, spare_table)
+        return experts_paired(hidden, normed, gate_code, up_proj, down_proj)
     experts = lax.axis_size("ep")
     tp_lanes = lax.axis_size("tp")
     per_row = routes.shape[1]

time: 190 us -> 128 us (0.67)
  the two profiles are of different devices: /device:TPU:9 before, /device:TPU:0 now
where the time goes in v2:
time: 128 us
  Pallas kernels  120 us (94%)
  other arithmetic  4.12 us (3%)
  local copies, waits for them, and re-layouts  2.97 us (2%)
    pallas_call x1, Pallas kernels, experts_paired(): pl.pallas_call(expert_kernel, out_shape=jax.ShapeDtypeStruct((rows, featu...  89.1 us
    pallas_call x1, Pallas kernels, attend_paired(): pl.pallas_call(attend_kernel, out_shape=(half, half), in_specs=[hbm, vmem...  30.8 us

profile of v2, /device:TPU:0, one launch (start us, length us, event | category | flops | bytes accessed | tf_op | source)
XLA Modules:
  0.0 127.6 jit_solution(2927510449447943377)
XLA Ops:
  0.7 1.4 %fusion.1 = s32[]{:T(128)} fusion(s32[8]{0:T(128)} %param.25, s32[]{:T(128)} %bitcast.4), kind=kLoop, calls=%fused_computation.6 | loop fusion | flops 23 | bytes 40 | tf_op jit(solution)/shard_map/reduce_sum | solution.py:605
  2.0 1.4 %compare_select_fusion = s32[32,3]{0,1:T(4,128)S(1)} fusion(s32[32,3]{0,1:T(4,128)} %param.22, s32[]{:T(128)} %fusion.1, s32[]{:T(128)} %bitcast.3), kind=kLoop, calls=%fused_computation.3 | loop fusion | flops 192 | bytes 776 | tf_op jit(solution)/shard_map/jit(_where)/select_n | solution.py:606
  3.4 0.8 select_reduce_fusion
  4.2 0.6 fusion.gate_code
  4.8 1.3 %reshape.33.gain = f32[1,3584]{1,0:T(1,128)} reshape(f32[3584]{0:T(1024)} %param.19) | data formatting | bytes 28672 | tf_op jit(solution)/shard_map/reshape | solution.py:238
  6.1 30.8 %shard_map.127 = (bf16[32,3584]{1,0:T(8,128)(2,1)}, bf16[32,3584]{1,0:T(8,128)(2,1)}) custom-call(bf16[2,32,4096]{2,1,0:T(8,128)(2,1)} %bitcast.5, bf16[2,32,512]{2,1,0:T(8,128)(2,1)} %bitcast.6, bf16[8,256,512]{2,1,0:T(8,128)(2,1)} %kv.1, s32[16]{0:T(128)} %lengths.1, bf16[32,3584]{1,0:T(8,128)(2,1)} %residual.1, bf16[4096,3584]{1,0:T(8,128)(2,1)} %w.1, ...), custom_call_target="tpu_custom_call" | custom-call | tf_op jit(solution)/shard_map/pallas_call | solution.py:197
  36.9 89.1 %shard_map.128 = bf16[32,3584]{1,0:T(8,128)(2,1)} custom-call(bf16[32,3584]{1,0:T(8,128)(2,1)} %get-tuple-element.7.hidden, bf16[32,3584]{1,0:T(8,128)(2,1)} %get-tuple-element.8.normed, bf16[32,128]{1,0:T(8,128)(2,1)} %fusion.gate_code, bf16[1,3584,1280]{2,1,0:T(8,128)(2,1)} %up.1, bf16[1,1280,3584]{2,1,0:T(8,128)(2,1)} %down.1), custom_call_target="tpu_custom_call" | custom-call | tf_op jit(solution)/shard_map/pallas_call | solution.py:558
  125.9 1.6 %copy.18 = bf16[32,3584]{1,0:T(8,128)(2,1)} copy(bf16[32,3584]{1,0:T(8,128)(2,1)} %shard_map.128) | data formatting | bytes 458752
  (2 shorter events, 0.0 us)

commit v3 on v2

--- a/solution.py
+++ b/solution.py
@@ -183,7 +183,7 @@
     for n in range(tiles):
         lanes = slice(n * TILE, (n + 1) * TILE)
         normed_out[:, lanes] = (
-            hidden_out[:, lanes].astype(jnp.float32) * scale * gain[:, lanes]
+            hidden_out[:, lanes].astype(jnp.float32) * scale * gain[lanes][None, :]
         ).astype(jnp.bfloat16)
 
 
@@ -235,14 +235,17 @@
         lengths,
         residual,
         out_proj,
-        norm_gain.reshape(1, features),
+        norm_gain,
     )
 
 
 def expert_kernel(
     hidden,
     normed,
-    gate_code,
+    routes,
+    route_gates,
+    lost_device,
+    spare_table,
     up,
     down,
     out,
@@ -310,7 +313,22 @@
 
     xa[z, c, tx] = normed[:, :width_a]
     xb[z, c, tx, :, :width_b] = normed[:, width_a:]
-    xb[z, c, tx, :, width_b:] = gate_code[...]
+    lost_id = lost_device[0]
+    spare_id = spare_table[0]
+    for e in range(1, spare_table.shape[0]):
+        spare_id = jnp.where(lost_id == e, spare_table[e], spare_id)
+    target = jnp.where(routes[...] == lost_id, spare_id, routes[...])
+    wide_lane = lax.broadcasted_iota(jnp.int32, (rows, 128), 1)
+    gates = jnp.zeros((rows, 128), jnp.float32)
+    for k in range(routes.shape[1]):
+        gates += jnp.where(
+            target[:, k : k + 1] == wide_lane % 64, route_gates[:, k : k + 1], 0.0
+        )
+    upper = gates.astype(jnp.bfloat16)
+    lower = gates - upper.astype(jnp.float32)
+    xb[z, c, tx, :, width_b:] = jnp.where(
+        wide_lane < 64, upper.astype(jnp.float32), lower
+    ).astype(jnp.bfloat16)
     barrier = pltpu.get_barrier_semaphore()
     for place, condition in zip(places, conditions):
         when(
@@ -454,6 +472,44 @@
         start(None, functools.partial(side_copy, zk))
         core_copy(0, zk).wait_recv()
 
+    arrivals = ((below_a, below_b, below_recv), (above_a, above_b, above_recv))
+
+    def chain_copy(part, way, zb):
+        return remote(
+            (chain_a, chain_b)[part].at[zb],
+            arrivals[way][part].at[zb],
+            chain_send.at[part, zb],
+            arrivals[way][2].at[part, zb],
+            way,
+        )
+
+    def own_a(zb):
+        return ya[zb, c].astype(f32) + core_a[zb].astype(f32)
+
+    def own_b(zb):
+        side_copy(zb).wait_recv()
+        return (
+            yb[zb, c, tx].astype(f32) + core_b[zb, tx].astype(f32) + side_in_b[zb].astype(f32)
+        )
+
+    def hop(way, zb, condition, joined):
+        def fill():
+            for part, held, own in ((0, chain_a, own_a), (1, chain_b, own_b)):
+                value = own(zb)
+                if joined:
+                    chain_copy(part, way, zb).wait_recv()
+                    value += arrivals[way][part][zb].astype(f32)
+                held[zb] = value.astype(jnp.bfloat16)
+                chain_copy(part, way, zb).start()
+
+        pl.when(condition)(fill)
+        for part in (0, 1):
+            pending.append((condition, functools.partial(chain_copy, part, way, zb)))
+
+    def depart(zb):
+        hop(0, zb, z == 0, False)
+        hop(1, zb, z == levels - 1, False)
+
     order = (z, z + 1 - 2 * (z % 2), (z + 2) % 4, 3 - z)
     for k in range(levels):
         phase(k)
@@ -465,50 +521,21 @@
             start(None, functools.partial(core_copy, part, order[k]))
         if k > 0:
             settle(order[k - 1])
+        if k > 1:
+            depart(order[k - 1])
     settle(order[levels - 1])
-
-    arrivals = ((below_a, below_b, below_recv), (above_a, above_b, above_recv))
-
-    def chain_copy(part, way, zb):
-        return remote(
-            (chain_a, chain_b)[part].at[zb],
-            arrivals[way][part].at[zb],
-            chain_send.at[part, zb],
-            arrivals[way][2].at[part, zb],
-            way,
-        )
-
-    def own_a(zb):
-        return ya[zb, c].astype(f32) + core_a[zb].astype(f32)
-
-    def own_b(zb):
-        side_copy(zb).wait_recv()
-        return (
-            yb[zb, c, tx].astype(f32) + core_b[zb, tx].astype(f32) + side_in_b[zb].astype(f32)
-        )
-
-    for d in range(levels - 1, 0, -1):
-        for way, zb, valid, joined in (
-            (0, z + d, z + d < levels, has_down),
-            (1, z - d, z >= d, has_up),
-        ):
-
-            def hop(way=way, zb=zb, joined=joined):
-                chain_a[zb] = own_a(zb).astype(jnp.bfloat16)
-                chain_b[zb] = own_b(zb).astype(jnp.bfloat16)
-
-                def join():
-                    for part, held in ((0, chain_a), (1, chain_b)):
-                        chain_copy(part, way, zb).wait_recv()
-                        held[zb] = (
-                            held[zb].astype(f32) + arrivals[way][part][zb].astype(f32)
-                        ).astype(jnp.bfloat16)
-
-                pl.when(joined)(join)
-
-            pl.when(valid)(hop)
-            for part in (0, 1):
-                start(valid, functools.partial(chain_copy, part, way, zb))
+    depart(order[levels - 1])
+
+    low, high = z == 1, z == levels - 2
+    for way, d, condition in (
+        (0, 1, low),
+        (1, 1, high),
+        (0, 2, low),
+        (1, 2, high),
+        (1, 1, low),
+        (0, 1, high),
+    ):
+        hop(way, z + d if way == 0 else z - d, condition, True)
 
     last_a[...] = own_a(z)
     side = own_b(z)
@@ -542,7 +569,9 @@
         when(condition, lambda: build().wait_send())
 
 
-def experts_paired(hidden, normed, gate_code, up_proj, down_proj):
+def experts_paired(
+    hidden, normed, routes, route_gates, lost_device, spare_table, up_proj, down_proj
+):
     rows, features = hidden.shape
     inner = up_proj.shape[2]
     levels = lax.axis_size("ep") // 2
@@ -550,6 +579,7 @@
     width_b = features - width_a
     vmem = pl.BlockSpec(memory_space=pltpu.VMEM)
     hbm = pl.BlockSpec(memory_space=pl.ANY)
+    smem = pl.BlockSpec(memory_space=pltpu.SMEM)
     dma = pltpu.SemaphoreType.DMA
 
     def held(*shape, dtype=jnp.bfloat16):
@@ -558,7 +588,7 @@
     return pl.pallas_call(
         expert_kernel,
         out_shape=jax.ShapeDtypeStruct((rows, features), jnp.bfloat16),
-        in_specs=[vmem, vmem, vmem, hbm, hbm],
+        in_specs=[vmem, vmem, vmem, vmem, smem, smem, hbm, hbm],
         out_specs=vmem,
         scratch_shapes=[
             held(levels, 2, 2, rows, width_a),
@@ -596,20 +626,7 @@
         compiler_params=pltpu.CompilerParams(
             collective_id=1, has_side_effects=True, vmem_limit_bytes=60 * 1024 * 1024
         ),
-    )(hidden, normed, gate_code, up_proj, down_proj)
-
-
-def code_gates(routes, route_gates, lost_device, spare_table):
-    experts = lax.axis_size("ep")
-    lost_id = lost_device[0]
-    spare_id = jnp.sum(jnp.where(jnp.arange(experts) == lost_id, spare_table, 0))
-    target = jnp.where(routes == lost_id, spare_id, routes)
-    lane = jnp.arange(128)[None, None, :]
-    gates = jnp.sum(
-        jnp.where(target[:, :, None] == lane % 64, route_gates[:, :, None], 0.0), axis=1
-    )
-    high = lax.reduce_precision(gates, 8, 7)
-    return jnp.where(lane[0] < 64, high, gates - high).astype(jnp.bfloat16)
+    )(hidden, normed, routes, route_gates, lost_device, spare_table, up_proj, down_proj)
 
 
 def attend_general(queries, draft_kv, kv_cache, lengths, residual, out_proj, norm_gain):
@@ -691,8 +708,9 @@
     )
     widened = hidden.astype(jnp.float32)
     if paired and lax.axis_size("ep") == 8 and kept_rows % 16 == 0:
-        gate_code = code_gates(routes, route_gates, lost_device, spare_table)
-        return experts_paired(hidden, normed, gate_code, up_proj, down_proj)
+        return experts_paired(
+            hidden, normed, routes, route_gates, lost_device, spare_table, up_proj, down_proj
+        )
     experts = lax.axis_size("ep")
     tp_lanes = lax.axis_size("tp")
     per_row = routes.shape[1]

time: 128 us -> 125 us (0.977)
  other arithmetic: 4.12 us -> 0 us
  local copies, waits for them, and re-layouts: 2.97 us -> 4.37 us
    unnamed x1 -> x3, local copies, waits for them, and re-layouts: 1.64 us -> 4.37 us
    reduce_sum x2 -> x0, other arithmetic: 2.14 us -> none  [the longest x1 1.37 us: code_gates(): jnp.sum(jnp.where(jnp.arange(experts) == lost_id, spare_table, 0))]
    select_n x2 -> x0, other arithmetic: 1.38 us -> none  [the longest x1 1.37 us: code_gates(): target = jnp.where(routes == lost_id, spare_id, routes)]
    reshape x1 -> x0, local copies, waits for them, and re-layouts: 1.33 us -> none  [attend_paired(): norm_gain.reshape(1, features)]
where the time goes in v3:
time: 125 us
  Pallas kernels  120 us (96%)
  local copies, waits for them, and re-layouts  4.37 us (3%)
    pallas_call x1, Pallas kernels, experts_paired(): pl.pallas_call(expert_kernel, out_shape=jax.ShapeDtypeStruct((rows, featu...  89 us
    pallas_call x1, Pallas kernels, attend_paired(): pl.pallas_call(attend_kernel, out_shape=(half, half), in_specs=[hbm, vmem...  30.8 us
    unnamed x3, local copies, waits for them, and re-layouts  4.37 us

profile of v3, /device:TPU:0, one launch (start us, length us, event | category | flops | bytes accessed | tf_op | source)
XLA Modules:
  0.0 124.8 jit_solution(9035341234251585064)
XLA Ops:
  0.7 1.4 %copy.14.routes = s32[32,3]{1,0:T(8,128)} copy(s32[32,3]{0,1:T(4,128)} %param.22) | data formatting | bytes 768 | tf_op args[9]
  2.0 1.4 %copy.15.route_gates = f32[32,3]{1,0:T(8,128)} copy(f32[32,3]{0,1:T(4,128)} %param.23) | data formatting | bytes 768 | tf_op args[10]
  3.4 30.8 %shard_map.127 = (bf16[32,3584]{1,0:T(8,128)(2,1)}, bf16[32,3584]{1,0:T(8,128)(2,1)}) custom-call(bf16[2,32,4096]{2,1,0:T(8,128)(2,1)} %bitcast.2, bf16[2,32,512]{2,1,0:T(8,128)(2,1)} %bitcast.3, bf16[8,256,512]{2,1,0:T(8,128)(2,1)} %kv.1, s32[16]{0:T(128)} %lengths.1, bf16[32,3584]{1,0:T(8,128)(2,1)} %residual.1, bf16[4096,3584]{1,0:T(8,128)(2,1)} %w.1, ...), custom_call_target="tpu_custom_call" | custom-call | tf_op jit(solution)/shard_map/pallas_call | solution.py:197
  34.1 89.0 %shard_map.128 = bf16[32,3584]{1,0:T(8,128)(2,1)} custom-call(bf16[32,3584]{1,0:T(8,128)(2,1)} %get-tuple-element.7.hidden, bf16[32,3584]{1,0:T(8,128)(2,1)} %get-tuple-element.8.normed, s32[32,3]{1,0:T(8,128)} %copy.14.routes, f32[32,3]{1,0:T(8,128)} %copy.15.route_gates, s32[1]{0:T(128)S(6)} %copy.17.lost_device, s32[8]{0:T(128)} %spare_table.1, ...), custom_call_target="tpu_custom_call" | custom-call | tf_op jit(solution)/shard_map/pallas_call | solution.py:588
  123.1 1.6 %copy.18 = bf16[32,3584]{1,0:T(8,128)(2,1)} copy(bf16[32,3584]{1,0:T(8,128)(2,1)} %shard_map.128) | data formatting | bytes 458752
